TPU v7x, 256 devices: a whole 4x4x8 slice. The times are simulated.
256 devices in a mesh: rep: 32 (over z_lo, y, core), fsdp: 8 (over z_hi, x).
Axes of the slice: x: 4, y: 4, z: 8 (z_hi: 2, z_lo: 4; z = z_hi * 4 + z_lo), core: 2. Of those that a mesh axis runs over, the one named last changes fastest.
Arguments:
- params: bfloat16 [32, 7168, 2048], P('rep', 'fsdp'), may hold values from -6 to 6
- hidden_acts: bfloat16 [32, 1024, 7168], P('rep', 'fsdp'), may hold values from -6 to 6
- out_grads: bfloat16 [32, 1024, 2048], P('rep', 'fsdp'), may hold values from -6 to 6
- step_counts: int32 [32], P('rep'), may hold values from 1 to 32
- outer_z: float32 [7168, 2048], P('fsdp', 'rep'), may hold values from -4 to 4
- outer_x: float32 [7168, 2048], P('fsdp', 'rep'), may hold values from -4 to 4
Outputs:
- new_z: float32 [7168, 2048], P('fsdp', 'rep')
- new_x: float32 [7168, 2048], P('fsdp', 'rep')
- new_y: bfloat16 [7168, 2048], P('fsdp')
All inputs are finite; a program needn't handle non-finite values.
Results may differ from a plain program's by a relative error of at most 0.0055.
Values may be sent and summed in bfloat16 or wider, within the bound.
A program may use at most 128 MiB of HBM per device.

v0:
```python
import jax
import jax.numpy as jnp
from jax import lax
from jax.sharding import Mesh
from jax.sharding import PartitionSpec as P

ROUND = 3
FSDP = ("fsdp_0", "fsdp_1")


def in_order(parts, dim):
    shape = list(parts.shape[1:])
    shape[dim] *= parts.shape[0]
    return jnp.moveaxis(parts, 0, dim).reshape(shape)


def all_blocks(array, axes, sequence):
    parts = array
    for k in sequence:
        parts = lax.all_gather(parts, axes[k])
    done = sequence[::-1]
    back = [done.index(k) for k in range(len(axes))]
    parts = parts.transpose(*back, *range(len(axes), parts.ndim))
    return parts.reshape(-1, *array.shape)


def gathered_by_axis(array, axes, sequence, dim):
    return in_order(all_blocks(array, axes, sequence), dim)


def sent_to_all(array, axis):
    copies = jnp.broadcast_to(array, (lax.axis_size(axis), *array.shape))
    return lax.all_to_all(copies, axis, split_axis=0, concat_axis=0, tiled=True)


def collect(array, axis, dim):
    parts = sent_to_all(array, axis)
    return in_order(parts, dim)


def transposed_product(left, right):
    return lax.dot_general(
        left, right, (((0,), (0,)), ((), ())), preferred_element_type=jnp.float32
    )


def local(params, hidden_acts, out_grads, step_counts, outer_z, outer_x):
    rows = params.shape[1]
    hidden_cols = lax.all_to_all(hidden_acts[0], FSDP, split_axis=1, concat_axis=0, tiled=True)
    grad = transposed_product(hidden_cols, gathered_by_axis(out_grads[0], FSDP, (0, 1), 0))
    inner = (params[0].astype(jnp.float32) - 0.1 * grad).astype(jnp.bfloat16)
    every_count = collect(step_counts, "rep", 0)
    replicas = every_count.shape[0]
    blocks = lax.all_to_all(inner, "rep", split_axis=1, concat_axis=0, tiled=True)
    columns = blocks.shape[1]
    stacked = blocks.reshape(replicas, rows * columns)
    weights = every_count.astype(jnp.bfloat16).reshape(1, replicas)
    summed = jnp.dot(weights, stacked, preferred_element_type=jnp.float32).reshape(rows, columns)
    total_f = jnp.sum(every_count).astype(jnp.float32)
    anchor = 0.1 * outer_z + 0.9 * outer_x
    pseudo = anchor - summed / total_f
    new_z = outer_z - 0.7 * pseudo
    mixing = 1.0 / (ROUND + 1.0)
    new_x = (1.0 - mixing) * outer_x + mixing * new_z
    block_y = (0.1 * new_z + 0.9 * new_x).astype(jnp.bfloat16)
    new_y = lax.all_gather(block_y, "rep", axis=1, tiled=True)
    return (new_z, new_x, new_y)


def solution(mesh):
    split = Mesh(mesh.devices.reshape(mesh.shape["rep"], 2, 4), ("rep", "fsdp_0", "fsdp_1"))
    placed = (
        P("rep", FSDP, None),
        P("rep", FSDP, None),
        P("rep", FSDP, None),
        P("rep"),
        P(FSDP, "rep"),
        P(FSDP, "rep"),
    )
    return jax.shard_map(
        local,
        mesh=split,
        in_specs=placed,
        out_specs=(P(FSDP, "rep"), P(FSDP, "rep"), P(FSDP, None)),
        check_vma=False,
    )
```

profile of v0, /device:TPU:1, one launch (start us, length us, event | category | flops | bytes accessed | tf_op | source)
XLA Modules:
  0.0 332.2 jit_solution(4786897905896339161)
XLA Ops:
  7.2 0.0 all-gather.5.cloned.1.call-start
  7.2 0.7 all-gather.5.cloned.1.call-update
  7.9 0.0 all-gather.9.cloned.1.call-start
  7.9 47.6 %all-gather.5.cloned.1.call-done = bf16[2,128,2048]{2,1,0:T(8,128)(2,1)} async-done(((bf16[1,128,2048]{2,1,0:T(8,128)(2,1)}), bf16[2,128,2048]{2,1,0:T(8,128)(2,1)}) %all-gather.5.cloned.1.call-update) | async-done | bytes 1048592 | tf_op jit(solution)/shard_map/all_gather | solution.py:20
  55.6 0.0 all-gather.9.cloned.1.call-update
  55.6 3.9 %copy.40 = bf16[1,128,7168]{1,2,0:T(8,128)(2,1)} copy(bf16[1,128,7168]{2,1,0:T(8,128)(2,1)} %param.7) | data formatting | bytes 3670016 | tf_op args[1]
  59.5 4.0 %all-to-all-start = ((bf16[128,8,896]{0,2,1:T(8,128)(2,1)}), bf16[128,8,896]{0,2,1:T(8,128)(2,1)S(1)}, u32[]{:S(2)}, u32[]{:S(2)}) async-start(bf16[128,8,896]{0,2,1:T(8,128)(2,1)} %bitcast.24), calls=%async_computation | async-start | bytes 3670016 | tf_op jit(solution)/shard_map/all_to_all | solution.py:49
  64.1 26.8 %all-to-all-done = bf16[128,8,896]{0,2,1:T(8,128)(2,1)S(1)} async-done(((bf16[128,8,896]{0,2,1:T(8,128)(2,1)}), bf16[128,8,896]{0,2,1:T(8,128)(2,1)S(1)}, u32[]{:S(2)}, u32[]{:S(2)}) %all-to-all-start) | async-done | bytes 1835040 | tf_op jit(solution)/shard_map/all_to_all | solution.py:49
  90.9 0.6 broadcast_in_dim.3
  91.5 25.4 %all-to-all-start.2 = ((s32[32,1,1]{2,1,0:T(1,128)}), s32[32,1,1]{2,1,0:T(1,128)S(1)}, u32[]{:S(2)}, u32[]{:S(2)}) async-start(s32[32,1,1]{2,1,0:T(1,128)} %broadcast_in_dim.3), calls=%async_computation.2 | async-start | bytes 32768 | tf_op jit(solution)/shard_map/all_to_all | solution.py:33
  116.9 2.6 copy.41
  119.5 1.8 all-gather.9.cloned.1.call-done
  121.3 2.7 copy.42
  123.9 0.1 copy-done
  124.0 1.1 copy-done.3
  125.1 5.7 %fusion = bf16[896,2048]{1,0:T(8,128)(2,1)} fusion(bf16[1024,896]{1,0:T(8,128)(2,1)S(1)} %bitcast.27, bf16[1024,2048]{1,0:T(8,128)(2,1)S(1)} %bitcast.26, bf16[1,896,2048]{2,1,0:T(8,128)(2,1)S(1)} %copy-done.3), kind=kOutput, calls=%fused_computation.2 | convolution fusion | flops 3765436416 | bytes 13369344 | tf_op jit(solution)/shard_map/dot_general | solution.py:42
  130.9 6.1 %copy.43 = bf16[896,2048]{0,1:T(8,128)(2,1)} copy(bf16[896,2048]{1,0:T(8,128)(2,1)} %fusion) | data formatting | bytes 7340032 | tf_op jit(solution)/shard_map/convert_element_type | solution.py:51
  136.9 0.0 all-to-all-done.2
  136.9 6.5 %all-to-all-start.1 = ((bf16[896,32,64]{0,2,1:T(8,128)(2,1)}), bf16[896,32,64]{0,2,1:T(8,128)(2,1)}, u32[]{:S(2)}, u32[]{:S(2)}) async-start(bf16[896,32,64]{0,2,1:T(8,128)(2,1)} %bitcast.21), calls=%async_computation.1 | async-start | bytes 7340032 | tf_op jit(solution)/shard_map/all_to_all | solution.py:54
  143.5 0.0 all-gather.7.cloned.1.call-start
  143.5 0.7 reduce_sum.9
  144.8 0.3 convert_reduce_fusion
  145.2 80.2 %all-to-all-done.1 = bf16[896,32,64]{0,2,1:T(8,128)(2,1)} async-done(((bf16[896,32,64]{0,2,1:T(8,128)(2,1)}), bf16[896,32,64]{0,2,1:T(8,128)(2,1)}, u32[]{:S(2)}, u32[]{:S(2)}) %all-to-all-start.1) | async-done | bytes 3670048 | tf_op jit(solution)/shard_map/all_to_all | solution.py:54
  225.4 7.8 %copy.44 = bf16[32,896,64]{2,1,0:T(8,128)(2,1)} copy(bf16[32,896,64]{1,2,0:T(8,128)(2,1)} %bitcast.9) | data formatting | bytes 7340032 | tf_op jit(solution)/shard_map/all_to_all | solution.py:54
  233.2 8.5 %reshape.37 = bf16[32,57344]{1,0:T(8,128)(2,1)} reshape(bf16[32,896,64]{2,1,0:T(8,128)(2,1)} %copy.44) | data formatting | bytes 7340032 | tf_op jit(solution)/shard_map/reshape | solution.py:56
  241.7 9.4 %dot_general.12 = bf16[896,64,32]{1,0,2:T(8,128)(2,1)} reshape(bf16[57344,32]{0,1:T(8,128)(2,1)} %bitcast.22) | data formatting | bytes 7340032 | tf_op jit(solution)/shard_map/dot_general | solution.py:58
  251.1 5.1 %multiply_reduce_fusion = f32[896,64]{1,0:T(8,128)S(1)} fusion(f32[32]{0:T(128)S(1)} %convert.2, bf16[896,64,32]{1,0,2:T(8,128)(2,1)} %dot_general.12), kind=kLoop, calls=%fused_computation | loop fusion | flops 5447680 | bytes 3899520
  256.2 0.2 copy.50
  256.4 0.9 add_convert_fusion
  257.3 0.0 all-gather.7.cloned.1.call-update
  257.3 62.3 %all-gather.7.cloned.1.call-done = bf16[896,2048]{0,1:T(8,128)(2,1)} async-done(((bf16[896,64]{0,1:T(8,128)(2,1)}), bf16[896,2048]{0,1:T(8,128)(2,1)}) %all-gather.7.cloned.1.call-update) | async-done | bytes 3670032 | tf_op jit(solution)/shard_map/all_gather | solution.py:66
  319.7 6.0 %copy.45 = bf16[896,2048]{1,0:T(8,128)(2,1)} copy(bf16[896,2048]{0,1:T(8,128)(2,1)} %all-gather.7.cloned.1.call-done) | data formatting | bytes 7340032
  (7 shorter events, 0.0 us)
Async XLA Ops:
  7.2 48.4 %all-gather.5.cloned.1.call-start = ((), (), s32[]{:S(2)}) async-start(), calls=%async_computation.3 | async-start | bytes 1572864 | tf_op jit(solution)/shard_map/all_gather | solution.py:20
  7.9 113.4 %all-gather.9.cloned.1.call-start = ((), (), s32[]{:S(2)}) async-start(), calls=%async_computation.5 | async-start | bytes 5242880 | tf_op jit(solution)/shard_map/all_gather | solution.py:20
  59.5 31.4 %all-to-all-start = ((bf16[128,8,896]{0,2,1:T(8,128)(2,1)}), bf16[128,8,896]{0,2,1:T(8,128)(2,1)S(1)}, u32[]{:S(2)}, u32[]{:S(2)}) async-start(bf16[128,8,896]{0,2,1:T(8,128)(2,1)} %bitcast.24), calls=%async_computation | async-start | bytes 3670016 | tf_op jit(solution)/shard_map/all_to_all | solution.py:49
  91.5 45.4 %all-to-all-start.2 = ((s32[32,1,1]{2,1,0:T(1,128)}), s32[32,1,1]{2,1,0:T(1,128)S(1)}, u32[]{:S(2)}, u32[]{:S(2)}) async-start(s32[32,1,1]{2,1,0:T(1,128)} %broadcast_in_dim.3), calls=%async_computation.2 | async-start | bytes 32768 | tf_op jit(solution)/shard_map/all_to_all | solution.py:33
  121.3 2.8 copy-start
  121.3 3.9 %copy-start.3 = (bf16[1,896,2048]{2,1,0:T(8,128)(2,1)S(1)}, bf16[1,896,2048]{2,1,0:T(8,128)(2,1)}, u32[]{:S(2)}) copy-start(bf16[1,896,2048]{2,1,0:T(8,128)(2,1)} %param.6) | copy-start | bytes 11010052
  136.9 88.5 %all-to-all-start.1 = ((bf16[896,32,64]{0,2,1:T(8,128)(2,1)}), bf16[896,32,64]{0,2,1:T(8,128)(2,1)}, u32[]{:S(2)}, u32[]{:S(2)}) async-start(bf16[896,32,64]{0,2,1:T(8,128)(2,1)} %bitcast.21), calls=%async_computation.1 | async-start | bytes 7340032 | tf_op jit(solution)/shard_map/all_to_all | solution.py:54
  143.5 176.2 %all-gather.7.cloned.1.call-start = ((), (), s32[]{:S(2)}) async-start(), calls=%async_computation.4 | async-start | bytes 3784704 | tf_op jit(solution)/shard_map/all_gather | solution.py:66
  251.1 5.3 %copy-start.1 = (f32[896,64]{0,1:T(8,128)S(1)}, f32[896,64]{0,1:T(8,128)}, u32[]{:S(2)}) copy-start(f32[896,64]{0,1:T(8,128)} %param.11) | copy-start | bytes 688132
  251.1 5.3 %copy-start.2 = (f32[896,64]{0,1:T(8,128)S(1)}, f32[896,64]{0,1:T(8,128)}, u32[]{:S(2)}) copy-start(f32[896,64]{0,1:T(8,128)} %param.10) | copy-start | bytes 688132
Sparse Core Ops, SparseCore 0:
  9.8 45.7 all-gather.4
  57.4 63.8 all-gather.8
  257.4 62.1 all-gather.6
where the time goes:
time: 333 us; the launch traced here: 332 us
  waiting for transfers between devices  219 us (66%)
  local copies, waits for them, and re-layouts  48.9 us (15%)
  starting transfers between devices  36 us (11%)
  between operations  15.1 us (5%)
  other arithmetic  7.03 us (2%)
  matrix products  5.74 us (2%)
    all_to_all x1, waiting for transfers between devices, local(): lax.all_to_all(inner, 'rep', split_axis=1, concat_axis=0, tiled=True)  80.2 us
    all_gather x1, waiting for transfers between devices, local(): new_y = lax.all_gather(block_y, 'rep', axis=1, tiled=True)  62.3 us
    all_gather x2, waiting for transfers between devices, all_blocks(): parts = lax.all_gather(parts, axes[k])  49.4 us
    all_to_all x1, waiting for transfers between devices, local(): lax.all_to_all(hidden_acts[0], FSDP, split_axis=1, concat_axis=0, tiled=T...  26.8 us
    all_to_all x1, starting transfers between devices, sent_to_all(): return lax.all_to_all(copies, axis, split_axis=0, concat_axis=0, tiled=True)  25.4 us
    unnamed x10, local copies, waits for them, and re-layouts  11.1 us
    dot_general x2, local copies, waits for them, and re-layouts, local(): jnp.dot(weights, stacked, preferred_element_type=jnp.float32)  9.55 us
    reshape x1, local copies, waits for them, and re-layouts, local(): stacked = blocks.reshape(replicas, rows * columns)  8.46 us
  transfers between devices with their start and end apart: 6, of which 5 were waited for; matrix products, arithmetic and copies ran while one was open for 7% of the time, Pallas kernels for 0%

commit v1 on v0

v1 whole, which is shorter than its diff:
```python
import functools

import jax
import jax.numpy as jnp
from jax import lax
from jax.experimental import pallas as pl
from jax.experimental.pallas import tpu as pltpu
from jax.sharding import Mesh
from jax.sharding import PartitionSpec as P

ROUND = 3
MESH = pl.DeviceIdType.MESH
CHUNKS = (128, 128, 128, 128, 128, 128, 128)
F32 = jnp.float32
BF16 = jnp.bfloat16


def kernel(
    p_ref, h_ref, g_ref, n_ref, z_ref, x_ref,
    zo_ref, xo_ref, yo_ref,
    hb, at, ab, gb, pb, wp, cb, r1a, r1b, r2a, r2b, zs, yg, yr, zt, xt, zf, xf, nzt, nxt, wt, ty, tz,
    in_sem, b_send, b_recv, sib_send, sib_recv, a_send, a_recv,
    y1_send, y1_recv, y2_send, y2_recv, z_send, z_recv, g1_send, g1_recv, g2_send, g2_recv,
    o_loc, o_send, o_recv, t_send, t_recv, e_send, e_recv,
):
    x, y, c = lax.axis_index("x"), lax.axis_index("y"), lax.axis_index("c")
    zh, zl = lax.axis_index("zh"), lax.axis_index("zl")
    z = zh * 4 + zl
    owner = zh == c
    other = 1 - c

    def plus(v, d, n=4):
        return lax.rem(v + d, n)

    def rdma(src, dst, ss, rs, **where):
        return pltpu.make_async_remote_copy(
            src_ref=src, dst_ref=dst, send_sem=ss, recv_sem=rs, device_id=where, device_id_type=MESH
        )

    def await_bytes(ref, sem):
        pltpu.make_async_copy(ref, ref, sem).wait()

    starts = [sum(CHUNKS[:m]) for m in range(len(CHUNKS))]
    rows_of = [slice(s, s + r) for s, r in zip(starts, CHUNKS)]
    n_chunks = len(CHUNKS)

    g_in = pltpu.make_async_copy(g_ref, gb.at[0, pl.ds(0, 128)], in_sem.at[0])
    g_in.start()
    h_in = pltpu.make_async_copy(h_ref, hb, in_sem.at[1])
    h_in.start()
    mine = pl.ds(pl.multiple_of(c * 64, 64), 64)
    theirs = pl.ds(pl.multiple_of(other * 64, 64), 64)
    z_in = pltpu.make_async_copy(z_ref, zt.at[mine], in_sem.at[2])
    z_in.start()
    x_in = pltpu.make_async_copy(x_ref, xt.at[mine], in_sem.at[3])
    x_in.start()
    p_in = pltpu.make_async_copy(p_ref, pb.at[0], in_sem.at[4])

    @pl.when(owner)
    def _():
        p_in.start()

    wt[0] = jnp.full((8, 128), n_ref[0].astype(F32), F32)

    barrier = pltpu.get_barrier_semaphore()
    peers = [{"c": other}]
    peers += [{"x": plus(x, d), "c": k} for d in (1, 2, 3) for k in (c, other)]
    peers += [{"y": plus(y, d)} for d in (1, 2, 3)]
    peers += [{"zh": plus(z, d, 8) // 4, "zl": plus(z, d, 4)} for d in range(1, 8)]
    for peer in peers:
        pl.semaphore_signal(barrier, inc=1, device_id=peer, device_id_type=MESH)
    pl.semaphore_wait(barrier, len(peers))

    xp, xm = plus(x, 1), plus(x, 3)
    g_in.wait()
    lo, hi = pl.ds(0, 64), pl.ds(64, 64)
    own_lo, own_hi = gb.at[0, pl.ds(0, 64)], gb.at[0, pl.ds(64, 64)]
    from_left = [gb.at[0, pl.ds(128, 64)], gb.at[0, pl.ds(192, 64)]]
    from_right = [gb.at[0, pl.ds(384, 64)], gb.at[0, pl.ds(448, 64)]]
    far = [gb.at[0, pl.ds(256, 64)], gb.at[0, pl.ds(320, 64)]]
    b_copies = [
        rdma(own_lo, from_left[0], b_send.at[0], b_recv.at[0], x=xp),
        rdma(own_hi, from_right[1], b_send.at[3], b_recv.at[3], x=xm),
        rdma(own_hi, from_left[1], b_send.at[1], b_recv.at[1], x=xp),
        rdma(own_lo, from_right[0], b_send.at[2], b_recv.at[2], x=xm),
    ]
    for copy in b_copies:
        copy.start()

    def to_sibling(k):
        part = pl.ds(k * 128, 128)
        return rdma(gb.at[0, part], gb.at[1, part], sib_send.at[k], sib_recv.at[k], c=other)

    w_copy = rdma(wt.at[0], wt.at[1], e_send.at[0], e_recv.at[0], c=other)
    w_copy.start()
    sib_copies = [to_sibling(k) for k in range(4)]
    sib_copies[0].start()
    p_copy = rdma(p_ref, pb.at[1], e_send.at[1], e_recv.at[1], c=other)

    @pl.when(jnp.logical_not(owner))
    def _():
        p_copy.start()

    z_copy = rdma(z_ref, zt.at[mine], e_send.at[2], e_recv.at[2], c=other)
    z_copy.start()
    x_copy = rdma(x_ref, xt.at[mine], e_send.at[3], e_recv.at[3], c=other)
    x_copy.start()

    h_in.wait()

    @pl.loop(0, 8)
    def _(q):
        for i in range(7):
            cols = pl.ds(pl.multiple_of(q * 896 + i * 128, 128), 128)
            at[q, i * 128 : (i + 1) * 128, :] = hb[:, cols].T

    w_copy.wait()
    ty[0] = wt[0] + wt[1]
    ty_copies = [rdma(ty.at[0], ty.at[d], t_send.at[d - 1], t_recv.at[d - 1], y=plus(y, d)) for d in (1, 2, 3)]
    for copy in ty_copies:
        copy.start()

    def send_inputs(m):
        r = rows_of[m]
        for dx in (2, 1, 3, 0):
            for dc in (0, 1):
                core = plus(c, dc, 2)
                to_x = plus(x, dx)
                src = at.at[core * 4 + to_x, r]
                dst = ab.at[r, pl.ds((dc * 4 + dx) * 128, 128)]
                if dx == 0 and dc == 0:
                    pltpu.make_async_copy(src, dst, a_recv.at[m]).start()
                else:
                    rdma(src, dst, a_send.at[m], a_recv.at[m], x=to_x, c=core).start()

    b_copies[0].wait_recv()
    fwd_a = rdma(from_left[0], far[0], b_send.at[4], b_recv.at[4], x=xp)
    fwd_a.start()
    b_copies[1].wait_recv()
    fwd_b = rdma(from_right[1], far[1], b_send.at[5], b_recv.at[5], x=xm)
    fwd_b.start()
    send_inputs(0)
    if n_chunks > 1:
        send_inputs(1)

    for copy in ty_copies:
        copy.wait()
    tz[0] = ty[0] + ty[1] + ty[2] + ty[3]
    tz_copies = [rdma(tz.at[0], tz.at[d], t_send.at[d + 2], t_recv.at[d + 2], zl=plus(zl, d)) for d in (1, 2, 3)]
    for copy in tz_copies:
        copy.start()

    w_own, w_sib = wt[0][0:1, :], wt[1][0:1, :]

    @pl.when(owner)
    def _():
        p_in.wait()
        p_copy.wait_recv()

        @pl.loop(0, 56)
        def _(i):
            r = pl.ds(pl.multiple_of(i * 16, 16), 16)
            for j in range(16):
                k = slice(j * 128, (j + 1) * 128)
                wp[r, k] = w_own * pb[0, r, k].astype(F32) + w_sib * pb[1, r, k].astype(F32)

    @pl.when(jnp.logical_not(owner))
    def _():
        p_copy.wait_send()

        @pl.loop(0, 56)
        def _(i):
            r = pl.ds(pl.multiple_of(i * 16, 16), 16)
            wp[r, :] = jnp.zeros((16, 2048), F32)

    z_in.wait()
    x_in.wait()
    z_copy.wait()
    x_copy.wait()
    for i in range(7):
        k = slice(i * 128, (i + 1) * 128)
        zf[k, :] = zt[:, k].T
        xf[k, :] = xt[:, k].T
    for copy in tz_copies:
        copy.wait()
    total = (tz[0] + tz[1] + tz[2] + tz[3])[0:1, :]

    b_copies[2].wait_recv()
    sib_copies[1].start()
    b_copies[3].wait_recv()
    sib_copies[3].start()
    fwd_a.wait_recv()
    fwd_b.wait_recv()
    sib_copies[2].start()
    for copy in sib_copies:
        copy.wait_recv()

    yp, ym, yf = plus(y, 1), plus(y, 3), plus(y, 2)

    def y_first(m):
        r = rows_of[m]
        return [
            rdma(cb.at[yf, pl.ds(0, 2), r], r1a.at[:, r], y1_send.at[m, 0], y1_recv.at[m, 0], y=yp),
            rdma(cb.at[yf, pl.ds(2, 2), r], r1b.at[:, r], y1_send.at[m, 1], y1_recv.at[m, 1], y=ym),
        ]

    def y_second(m):
        r = rows_of[m]
        return [
            rdma(cb.at[yp, :, r], r2a.at[:, r], y2_send.at[m, 0], y2_recv.at[m, 0], y=yp),
            rdma(cb.at[ym, :, r], r2b.at[:, r], y2_send.at[m, 1], y2_recv.at[m, 1], y=ym),
        ]

    def multiply(m):
        r = rows_of[m]
        await_bytes(ab.at[r], a_recv.at[m])
        if m + 2 < n_chunks:
            send_inputs(m + 2)

        @pl.loop(0, 4)
        def _(q):
            cols = pl.ds(pl.multiple_of(q * 512, 512), 512)
            d_own = jnp.dot(ab[r, 0:512], gb[0, :, cols], preferred_element_type=F32)
            d_sib = jnp.dot(ab[r, 512:1024], gb[1, :, cols], preferred_element_type=F32)
            for j in range(4):
                k = slice(j * 128, (j + 1) * 128)
                base = wp[r, pl.ds(pl.multiple_of(q * 512 + j * 128, 128), 128)]
                cb[j, q, r] = (base - 0.1 * (w_own * d_own[:, k] + w_sib * d_sib[:, k])).astype(BF16)

        for copy in y_first(m):
            copy.start()

    def merge(m):
        r = rows_of[m]
        first, second = y_first(m), y_second(m)
        first[0].wait_recv()
        for j in (0, 1):
            cb[yp, j, r] = (cb[yp, j, r].astype(F32) + r1a[j, r].astype(F32)).astype(BF16)
        second[0].start()
        first[1].wait_recv()
        for j in (2, 3):
            cb[ym, j, r] = (cb[ym, j, r].astype(F32) + r1b[j - 2, r].astype(F32)).astype(BF16)
        second[1].start()

    def z_copies(m):
        r = rows_of[m]
        return [
            rdma(cb.at[y, plus(zl, d), r], zs.at[z, r], z_send.at[m], z_recv.at[m], zh=c, zl=plus(zl, d))
            for d in range(4)
        ]

    def along_z(m):
        r = rows_of[m]
        for copy in y_second(m):
            copy.wait_recv()
        for j in range(4):
            cb[y, j, r] = (cb[y, j, r].astype(F32) + r2a[j, r].astype(F32) + r2b[j, r].astype(F32)).astype(BF16)
        copies = z_copies(m)
        for d in (2, 1, 3):
            copies[d].start()

        @pl.when(owner)
        def _():
            pltpu.make_async_copy(cb.at[y, zl, r], zs.at[z, r], z_recv.at[m]).start()

        @pl.when(jnp.logical_not(owner))
        def _():
            copies[0].start()

    def finish(m):
        r = rows_of[m]
        await_bytes(zs.at[:, r], z_recv.at[m])
        summed = zs[0, r].astype(F32)
        for k in range(1, 8):
            summed = summed + zs[k, r].astype(F32)
        outer_z, outer_x = zf[r, :], xf[r, :]
        anchor = 0.1 * outer_z + 0.9 * outer_x
        pseudo = anchor - summed / total
        new_z = outer_z - 0.7 * pseudo
        mixing = 1.0 / (ROUND + 1.0)
        new_x = (1.0 - mixing) * outer_x + mixing * new_z
        yg[y, zl, r] = (0.1 * new_z + 0.9 * new_x).astype(BF16)
        for d in (1, 2, 3):
            rdma(yg.at[y, zl, r], yg.at[y, zl, r], g1_send.at[m], g1_recv.at[m], zl=plus(zl, d)).start()
        nzt[:, r] = new_z.T
        nxt[:, r] = new_x.T

    def gather_y(m):
        r = rows_of[m]
        await_bytes(yg.at[y, pl.ds(0, 3), r], g1_recv.at[m])
        for d in (2, 1, 3):
            rdma(yg.at[y, :, r], yg.at[y, :, r], g2_send.at[m], g2_recv.at[m], y=plus(y, d)).start()

    def out_copies(m):
        r = rows_of[m]
        return (
            pltpu.make_async_copy(yr.at[r], yo_ref.at[r], o_loc.at[m]),
            rdma(yr.at[r], yo_ref.at[r], o_send.at[m], o_recv.at[m], c=other),
        )

    def deliver(m):
        r = rows_of[m]
        await_bytes(yg.at[pl.ds(0, 3), :, r], g2_recv.at[m])
        for j in range(16):
            yr[r, j * 128 : (j + 1) * 128] = yg[j % 4, j // 4, r]
        for copy in out_copies(m):
            copy.start()

    state_out = (
        pltpu.make_async_copy(nzt.at[mine], zo_ref, in_sem.at[5]),
        pltpu.make_async_copy(nxt.at[mine], xo_ref, in_sem.at[6]),
    )
    state_away = (
        rdma(nzt.at[theirs], zo_ref, e_send.at[4], e_recv.at[4], c=other),
        rdma(nxt.at[theirs], xo_ref, e_send.at[5], e_recv.at[5], c=other),
    )

    for t in range(n_chunks + 5):
        if t < n_chunks:
            multiply(t)
        if 0 <= t - 1 < n_chunks:
            merge(t - 1)
        if 0 <= t - 2 < n_chunks:
            along_z(t - 2)

        @pl.when(owner)
        def _():
            if 0 <= t - 3 < n_chunks:
                finish(t - 3)
            if t - 3 == n_chunks - 1:
                for copy in (*state_out, *state_away):
                    copy.start()
            if 0 <= t - 4 < n_chunks:
                gather_y(t - 4)
            if 0 <= t - 5 < n_chunks:
                deliver(t - 5)

    for copy in (*b_copies, fwd_a, fwd_b, *sib_copies):
        copy.wait_send()
    for m in range(n_chunks):
        r = rows_of[m]
        await_bytes(ab.at[r, pl.ds(0, 896)], a_send.at[m])
        for copy in (*y_first(m), *y_second(m)):
            copy.wait_send()

    @pl.when(owner)
    def _():
        for m in range(n_chunks):
            r = rows_of[m]
            await_bytes(zs.at[pl.ds(0, 3), r], z_send.at[m])
            await_bytes(yg.at[0, pl.ds(0, 3), r], g1_send.at[m])
            await_bytes(yg.at[pl.ds(0, 3), :, r], g2_send.at[m])
            here, away = out_copies(m)
            here.wait()
            away.wait_send()
        for copy in state_out:
            copy.wait()
        for copy in state_away:
            copy.wait_send()

    @pl.when(jnp.logical_not(owner))
    def _():
        for m in range(n_chunks):
            await_bytes(zs.at[pl.ds(0, 4), rows_of[m]], z_send.at[m])
            out_copies(m)[1].wait_recv()
        for copy in state_away:
            copy.wait_recv()


def local(params, hidden_acts, out_grads, step_counts, outer_z, outer_x):
    n = len(CHUNKS)
    dma = pltpu.SemaphoreType.DMA
    hbm = pl.BlockSpec(memory_space=pl.ANY)
    new_z, new_x, new_y = pl.pallas_call(
        kernel,
        name="outer_sync",
        out_shape=(
            jax.ShapeDtypeStruct((64, 896), F32),
            jax.ShapeDtypeStruct((64, 896), F32),
            jax.ShapeDtypeStruct((896, 2048), BF16),
        ),
        in_specs=[hbm, hbm, hbm, pl.BlockSpec(memory_space=pltpu.SMEM), hbm, hbm],
        out_specs=(hbm, hbm, hbm),
        scratch_shapes=[
            pltpu.VMEM((128, 7168), BF16),
            pltpu.VMEM((8, 896, 128), BF16),
            pltpu.VMEM((896, 1024), BF16),
            pltpu.VMEM((2, 512, 2048), BF16),
            pltpu.VMEM((2, 896, 2048), BF16),
            pltpu.VMEM((896, 2048), F32),
            pltpu.VMEM((4, 4, 896, 128), BF16),
            pltpu.VMEM((2, 896, 128), BF16),
            pltpu.VMEM((2, 896, 128), BF16),
            pltpu.VMEM((4, 896, 128), BF16),
            pltpu.VMEM((4, 896, 128), BF16),
            pltpu.VMEM((8, 896, 128), BF16),
            pltpu.VMEM((4, 4, 896, 128), BF16),
            pltpu.VMEM((896, 2048), BF16),
            pltpu.VMEM((128, 896), F32),
            pltpu.VMEM((128, 896), F32),
            pltpu.VMEM((896, 128), F32),
            pltpu.VMEM((896, 128), F32),
            pltpu.VMEM((128, 896), F32),
            pltpu.VMEM((128, 896), F32),
            pltpu.VMEM((2, 8, 128), F32),
            pltpu.VMEM((4, 8, 128), F32),
            pltpu.VMEM((4, 8, 128), F32),
            dma((7,)),
            dma((6,)), dma((6,)),
            dma((4,)), dma((4,)),
            dma((n,)), dma((n,)),
            dma((n, 2)), dma((n, 2)),
            dma((n, 2)), dma((n, 2)),
            dma((n,)), dma((n,)),
            dma((n,)), dma((n,)),
            dma((n,)), dma((n,)),
            dma((n,)), dma((n,)), dma((n,)),
            dma((6,)), dma((6,)),
            dma((6,)), dma((6,)),
        ],
        compiler_params=pltpu.CompilerParams(
            collective_id=0, has_side_effects=True, vmem_limit_bytes=60 * 2**20
        ),
        cost_estimate=pl.CostEstimate(flops=3_760_000_000, bytes_accessed=12_000_000, transcendentals=0),
    )(params[0], hidden_acts[0], out_grads[0], step_counts, outer_z.T, outer_x.T)
    return new_z.T, new_x.T, new_y


def solution(mesh):
    split = Mesh(mesh.devices.reshape(4, 4, 2, 2, 4), ("zl", "y", "c", "zh", "x"))
    rep, fsdp = ("zl", "y", "c"), ("zh", "x")
    placed = (
        P(rep, fsdp, None),
        P(rep, fsdp, None),
        P(rep, fsdp, None),
        P(rep),
        P(fsdp, rep),
        P(fsdp, rep),
    )
    return jax.shard_map(
        local,
        mesh=split,
        in_specs=placed,
        out_specs=(P(fsdp, rep), P(fsdp, rep), P(fsdp, None)),
        check_vma=False,
    )
```

time: 333 us -> 105 us (0.32)
  waiting for transfers between devices: 219 us -> 0 us
  Pallas kernels: 0 us -> 96 us
  local copies, waits for them, and re-layouts: 48.9 us -> 7.65 us
  starting transfers between devices: 36 us -> 0 us
  between operations: 15.1 us -> 1.29 us
  other arithmetic: 7.03 us -> 0 us
  matrix products: 5.74 us -> 0 us
    all_gather x3 -> x0, waiting for transfers between devices: 112 us -> none  [the longest x1 62.3 us: local(): new_y = lax.all_gather(block_y, 'rep', axis=1, tiled=True)]
    all_to_all x3 -> x0, waiting for transfers between devices: 107 us -> none  [the longest x1 80.2 us: local(): lax.all_to_all(inner, 'rep', split_axis=1, concat_axis=0, tiled=True)]
    pallas_call x0 -> x1, Pallas kernels: none -> 96 us  [local(): pl.pallas_call(kernel, name='outer_sync', out_shape=(jax.ShapeDtypeStruct...]
    all_to_all x3 -> x0, starting transfers between devices: 35.9 us -> none  [the longest x1 25.4 us: sent_to_all(): return lax.all_to_all(copies, axis, split_axis=0, concat_axis=0, tiled=True)]
    all_to_all x2 -> x0, local copies, waits for them, and re-layouts: 10.4 us -> none  [the longest x1 7.79 us: local(): lax.all_to_all(inner, 'rep', split_axis=1, concat_axis=0, tiled=True)]
    dot_general x2 -> x0, local copies, waits for them, and re-layouts: 9.55 us -> none  [local(): jnp.dot(weights, stacked, preferred_element_type=jnp.float32)]
    reshape x1 -> x0, local copies, waits for them, and re-layouts: 8.46 us -> none  [local(): stacked = blocks.reshape(replicas, rows * columns)]
    convert_element_type x1 -> x0, local copies, waits for them, and re-layouts: 6.06 us -> none  [local(): inner = (params[0].astype(jnp.float32) - 0.1 * grad).astype(jnp.bfloat16)]
  transfers between devices with their start and end apart: 6 -> 0, of which waited for: 5 -> 0; matrix products, arithmetic and copies ran while one was open for 7% -> 0% of each run, Pallas kernels for 0% -> 0%
where the time goes in v1:
time: 105 us
  Pallas kernels  96 us (91%)
  local copies, waits for them, and re-layouts  7.65 us (7%)
  between operations  1.29 us (1%)
    pallas_call x1, Pallas kernels, local(): pl.pallas_call(kernel, name='outer_sync', out_shape=(jax.ShapeDtypeStruct...  96 us
    unnamed x3, local copies, waits for them, and re-layouts  7.65 us

profile of v1, /device:TPU:1, one launch (start us, length us, event | category | flops | bytes accessed | tf_op | source)
XLA Modules:
  0.0 104.9 jit_solution(1610687654522273306)
XLA Ops:
  1.3 96.0 %outer_sync.1 = (f32[64,896]{1,0:T(8,128)}, f32[64,896]{1,0:T(8,128)}, bf16[896,2048]{1,0:T(8,128)(2,1)}) custom-call(bf16[896,2048]{1,0:T(8,128)(2,1)} %bitcast.9, bf16[128,7168]{1,0:T(8,128)(2,1)} %bitcast.10, bf16[128,2048]{1,0:T(8,128)(2,1)} %bitcast.11, s32[1]{0:T(128)S(6)} %copy.12.n_ref, f32[64,896]{1,0:T(8,128)} %bitcast.12, f32[64,896]{1,0:T(8,128)} %bitcast.13), custom_call_target="tpu_custom_call" | custom-call | flops 3760000000 | bytes 12000000 | tf_op jit(solution)/shard_map/outer_sync/pallas_call | solution.py:374
  97.3 1.6 %copy.13 = f32[896,64]{0,1:T(8,128)} copy(f32[896,64]{0,1:T(8,128)} %bitcast.8) | data formatting | bytes 458752
  98.9 1.6 %copy.14 = f32[896,64]{0,1:T(8,128)} copy(f32[896,64]{0,1:T(8,128)} %bitcast.7) | data formatting | bytes 458752
  100.6 4.4 %copy.15 = bf16[896,2048]{1,0:T(8,128)(2,1)} copy(bf16[896,2048]{1,0:T(8,128)(2,1)} %get-tuple-element.14) | data formatting | bytes 7340032

commit v2 on v1

--- a/solution.py
+++ b/solution.py
@@ -10,7 +10,10 @@
 
 ROUND = 3
 MESH = pl.DeviceIdType.MESH
-CHUNKS = (128, 128, 128, 128, 128, 128, 128)
+CHUNKS = (128, 128, 128, 128, 128, 128, 64, 64)
+SKEW = (1, 2, 3, 4, 5, 6)
+RELAY = (0, 1, 2, 3, 4, 5)
+Y_FIRST = ()
 F32 = jnp.float32
 BF16 = jnp.bfloat16
 
@@ -18,10 +21,10 @@
 def kernel(
     p_ref, h_ref, g_ref, n_ref, z_ref, x_ref,
     zo_ref, xo_ref, yo_ref,
-    hb, at, ab, gb, pb, wp, cb, r1a, r1b, r2a, r2b, zs, yg, yr, zt, xt, zf, xf, nzt, nxt, wt, ty, tz,
+    hb, at, ab, gb, pb, wp, cb, r1a, r1b, r2a, r2b, zs, yg, zt, xt, zf, xf, nzt, nxt, wt, ty, tz,
     in_sem, b_send, b_recv, sib_send, sib_recv, a_send, a_recv,
     y1_send, y1_recv, y2_send, y2_recv, z_send, z_recv, g1_send, g1_recv, g2_send, g2_recv,
-    o_loc, o_send, o_recv, t_send, t_recv, e_send, e_recv,
+    o_send, o_recv, t_send, t_recv, e_send, e_recv,
 ):
     x, y, c = lax.axis_index("x"), lax.axis_index("y"), lax.axis_index("c")
     zh, zl = lax.axis_index("zh"), lax.axis_index("zl")
@@ -84,7 +87,7 @@
         rdma(own_hi, from_left[1], b_send.at[1], b_recv.at[1], x=xp),
         rdma(own_lo, from_right[0], b_send.at[2], b_recv.at[2], x=xm),
     ]
-    for copy in b_copies:
+    for copy in b_copies[:2]:
         copy.start()
 
     def to_sibling(k):
@@ -108,11 +111,15 @@
 
     h_in.wait()
 
-    @pl.loop(0, 8)
-    def _(q):
+    def transpose(q):
         for i in range(7):
             cols = pl.ds(pl.multiple_of(q * 896 + i * 128, 128), 128)
             at[q, i * 128 : (i + 1) * 128, :] = hb[:, cols].T
+
+    pl.loop(0, 3)(transpose)
+    for copy in b_copies[2:]:
+        copy.start()
+    pl.loop(3, 8)(transpose)
 
     w_copy.wait()
     ty[0] = wt[0] + wt[1]
@@ -280,31 +287,47 @@
         mixing = 1.0 / (ROUND + 1.0)
         new_x = (1.0 - mixing) * outer_x + mixing * new_z
         yg[y, zl, r] = (0.1 * new_z + 0.9 * new_x).astype(BF16)
-        for d in (1, 2, 3):
-            rdma(yg.at[y, zl, r], yg.at[y, zl, r], g1_send.at[m], g1_recv.at[m], zl=plus(zl, d)).start()
-        nzt[:, r] = new_z.T
-        nxt[:, r] = new_x.T
+        for d in (2, 1, 3):
+            where = {"y": plus(y, d)} if m in Y_FIRST else {"zl": plus(zl, d)}
+            rdma(yg.at[y, zl, r], yg.at[y, zl, r], g1_send.at[m], g1_recv.at[m], **where).start()
+        zf[r, :] = new_z
+        xf[r, :] = new_x
 
     def gather_y(m):
         r = rows_of[m]
         await_bytes(yg.at[y, pl.ds(0, 3), r], g1_recv.at[m])
-        for d in (2, 1, 3):
-            rdma(yg.at[y, :, r], yg.at[y, :, r], g2_send.at[m], g2_recv.at[m], y=plus(y, d)).start()
-
-    def out_copies(m):
-        r = rows_of[m]
-        return (
-            pltpu.make_async_copy(yr.at[r], yo_ref.at[r], o_loc.at[m]),
-            rdma(yr.at[r], yo_ref.at[r], o_send.at[m], o_recv.at[m], c=other),
-        )
+        if m in Y_FIRST:
+            part, steps = yg.at[:, zl, r], [({"zl": plus(zl, d)}, 0) for d in (2, 1, 3)]
+        elif m in RELAY:
+            part, steps = yg.at[y, :, r], [({"y": yp}, 0), ({"y": ym}, 1)]
+        else:
+            part, steps = yg.at[y, :, r], [({"y": plus(y, d)}, 0) for d in (2, 1, 3)]
+        for where, k in steps:
+            rdma(part, part, g2_send.at[m], g2_recv.at[m, k], **where).start()
+
+    def pass_y(m):
+        r = rows_of[m]
+        await_bytes(yg.at[ym, :, r], g2_recv.at[m, 0])
+        part = yg.at[ym, pl.ds(0, 2), r]
+        rdma(part, part, g2_send.at[m], g2_recv.at[m, 2], y=yp).start()
+        await_bytes(yg.at[yp, :, r], g2_recv.at[m, 1])
+        part = yg.at[yp, pl.ds(2, 2), r]
+        rdma(part, part, g2_send.at[m], g2_recv.at[m, 3], y=ym).start()
+
+    def out_away(m):
+        r = rows_of[m]
+        return rdma(yo_ref.at[r], yo_ref.at[r], o_send.at[m], o_recv.at[m], c=other)
 
     def deliver(m):
         r = rows_of[m]
-        await_bytes(yg.at[pl.ds(0, 3), :, r], g2_recv.at[m])
+        if m in RELAY:
+            await_bytes(yg.at[yf, pl.ds(0, 2), r], g2_recv.at[m, 2])
+            await_bytes(yg.at[yf, pl.ds(2, 2), r], g2_recv.at[m, 3])
+        else:
+            await_bytes(yg.at[pl.ds(0, 3), :, r], g2_recv.at[m, 0])
         for j in range(16):
-            yr[r, j * 128 : (j + 1) * 128] = yg[j % 4, j // 4, r]
-        for copy in out_copies(m):
-            copy.start()
+            yo_ref[r, j * 128 : (j + 1) * 128] = yg[j % 4, j // 4, r]
+        out_away(m).start()
 
     state_out = (
         pltpu.make_async_copy(nzt.at[mine], zo_ref, in_sem.at[5]),
@@ -315,25 +338,33 @@
         rdma(nxt.at[theirs], xo_ref, e_send.at[5], e_recv.at[5], c=other),
     )
 
-    for t in range(n_chunks + 5):
-        if t < n_chunks:
+    s_merge, s_along, s_finish, s_gather, s_pass, s_deliver = SKEW
+    chunks = range(n_chunks)
+    for t in range(n_chunks + s_deliver):
+        if t in chunks:
             multiply(t)
-        if 0 <= t - 1 < n_chunks:
-            merge(t - 1)
-        if 0 <= t - 2 < n_chunks:
-            along_z(t - 2)
+        if t - s_merge in chunks:
+            merge(t - s_merge)
+        if t - s_along in chunks:
+            along_z(t - s_along)
 
         @pl.when(owner)
         def _():
-            if 0 <= t - 3 < n_chunks:
-                finish(t - 3)
-            if t - 3 == n_chunks - 1:
+            if t - s_finish in chunks:
+                finish(t - s_finish)
+            if t - s_gather in chunks:
+                gather_y(t - s_gather)
+            if t - s_finish == n_chunks - 1:
+                for i in range(7):
+                    k = slice(i * 128, (i + 1) * 128)
+                    nzt[:, k] = zf[k, :].T
+                    nxt[:, k] = xf[k, :].T
                 for copy in (*state_out, *state_away):
                     copy.start()
-            if 0 <= t - 4 < n_chunks:
-                gather_y(t - 4)
-            if 0 <= t - 5 < n_chunks:
-                deliver(t - 5)
+            if t - s_pass in chunks and t - s_pass in RELAY:
+                pass_y(t - s_pass)
+            if t - s_deliver in chunks:
+                deliver(t - s_deliver)
 
     for copy in (*b_copies, fwd_a, fwd_b, *sib_copies):
         copy.wait_send()
@@ -350,9 +381,7 @@
             await_bytes(zs.at[pl.ds(0, 3), r], z_send.at[m])
             await_bytes(yg.at[0, pl.ds(0, 3), r], g1_send.at[m])
             await_bytes(yg.at[pl.ds(0, 3), :, r], g2_send.at[m])
-            here, away = out_copies(m)
-            here.wait()
-            away.wait_send()
+            out_away(m).wait_send()
         for copy in state_out:
             copy.wait()
         for copy in state_away:
@@ -362,7 +391,7 @@
     def _():
         for m in range(n_chunks):
             await_bytes(zs.at[pl.ds(0, 4), rows_of[m]], z_send.at[m])
-            out_copies(m)[1].wait_recv()
+            out_away(m).wait_recv()
         for copy in state_away:
             copy.wait_recv()
 
@@ -371,16 +400,13 @@
     n = len(CHUNKS)
     dma = pltpu.SemaphoreType.DMA
     hbm = pl.BlockSpec(memory_space=pl.ANY)
+    vmem = pl.BlockSpec(memory_space=pltpu.VMEM)
     new_z, new_x, new_y = pl.pallas_call(
         kernel,
         name="outer_sync",
-        out_shape=(
-            jax.ShapeDtypeStruct((64, 896), F32),
-            jax.ShapeDtypeStruct((64, 896), F32),
-            jax.ShapeDtypeStruct((896, 2048), BF16),
-        ),
+        out_shape=(pltpu.VMEM((64, 896), F32), pltpu.VMEM((64, 896), F32), pltpu.VMEM((896, 2048), BF16)),
         in_specs=[hbm, hbm, hbm, pl.BlockSpec(memory_space=pltpu.SMEM), hbm, hbm],
-        out_specs=(hbm, hbm, hbm),
+        out_specs=(vmem, vmem, vmem),
         scratch_shapes=[
             pltpu.VMEM((128, 7168), BF16),
             pltpu.VMEM((8, 896, 128), BF16),
@@ -395,7 +421,6 @@
             pltpu.VMEM((4, 896, 128), BF16),
             pltpu.VMEM((8, 896, 128), BF16),
             pltpu.VMEM((4, 4, 896, 128), BF16),
-            pltpu.VMEM((896, 2048), BF16),
             pltpu.VMEM((128, 896), F32),
             pltpu.VMEM((128, 896), F32),
             pltpu.VMEM((896, 128), F32),
@@ -413,13 +438,13 @@
             dma((n, 2)), dma((n, 2)),
             dma((n,)), dma((n,)),
             dma((n,)), dma((n,)),
+            dma((n,)), dma((n, 4)),
             dma((n,)), dma((n,)),
-            dma((n,)), dma((n,)), dma((n,)),
             dma((6,)), dma((6,)),
             dma((6,)), dma((6,)),
         ],
         compiler_params=pltpu.CompilerParams(
-            collective_id=0, has_side_effects=True, vmem_limit_bytes=60 * 2**20
+            collective_id=0, has_side_effects=True, vmem_limit_bytes=50 * 2**20
         ),
         cost_estimate=pl.CostEstimate(flops=3_760_000_000, bytes_accessed=12_000_000, transcendentals=0),
     )(params[0], hidden_acts[0], out_grads[0], step_counts, outer_z.T, outer_x.T)

time: 105 us -> 98.9 us (0.942)
  local copies, waits for them, and re-layouts: 7.65 us -> 3.21 us
  Pallas kernels: 96 us -> 94.3 us
    unnamed x3, local copies, waits for them, and re-layouts: 7.65 us -> 3.21 us
    pallas_call x1, Pallas kernels: 96 us -> 94.3 us  [local(): pl.pallas_call(kernel, name='outer_sync', out_shape=(pltpu.VMEM((64, 896)...]
where the time goes in v2:
time: 98.9 us; the launch traced here: 98.8 us
  Pallas kernels  94.3 us (95%)
  local copies, waits for them, and re-layouts  3.21 us (3%)
  between operations  1.29 us (1%)
    pallas_call x1, Pallas kernels, local(): pl.pallas_call(kernel, name='outer_sync', out_shape=(pltpu.VMEM((64, 896)...  94.3 us
    unnamed x3, local copies, waits for them, and re-layouts  3.21 us

profile of v2, /device:TPU:1, one launch (start us, length us, event | category | flops | bytes accessed | tf_op | source)
XLA Modules:
  0.0 98.8 jit_solution(16874012850632729928)
XLA Ops:
  1.3 94.3 %outer_sync.1 = (f32[64,896]{1,0:T(8,128)S(1)}, f32[64,896]{1,0:T(8,128)S(1)}, bf16[896,2048]{1,0:T(8,128)(2,1)S(1)}) custom-call(bf16[896,2048]{1,0:T(8,128)(2,1)} %bitcast.9, bf16[128,7168]{1,0:T(8,128)(2,1)} %bitcast.10, bf16[128,2048]{1,0:T(8,128)(2,1)} %bitcast.11, s32[1]{0:T(128)S(6)} %copy.15.n_ref, f32[64,896]{1,0:T(8,128)} %bitcast.12, ...), custom_call_target="tpu_custom_call" | custom-call | flops 3760000000 | bytes 12000000 | tf_op jit(solution)/shard_map/outer_sync/pallas_call | solution.py:404
  95.5 0.7 copy.12
  96.2 0.7 copy.13
  96.9 1.8 %copy.14 = bf16[896,2048]{1,0:T(8,128)(2,1)} copy(bf16[896,2048]{1,0:T(8,128)(2,1)S(1)} %get-tuple-element.11) | data formatting | bytes 7340032

commit v3 on v2

--- a/solution.py
+++ b/solution.py
@@ -11,7 +11,8 @@
 ROUND = 3
 MESH = pl.DeviceIdType.MESH
 CHUNKS = (128, 128, 128, 128, 128, 128, 64, 64)
-SKEW = (1, 2, 3, 4, 5, 6)
+READY = {"multiply": 0, "merge": 1.01, "along_z": 2.02, "finish": 3.03, "gather_y": 4.04, "pass_y": 5.05, "deliver": 6.06}
+AHEAD = 2
 RELAY = (0, 1, 2, 3, 4, 5)
 Y_FIRST = ()
 F32 = jnp.float32
@@ -66,10 +67,10 @@
     wt[0] = jnp.full((8, 128), n_ref[0].astype(F32), F32)
 
     barrier = pltpu.get_barrier_semaphore()
-    peers = [{"c": other}]
+    peers = [{"zh": plus(z, d, 8) // 4, "zl": plus(z, d, 4)} for d in (4, 3, 5, 2, 6, 1, 7)]
     peers += [{"x": plus(x, d), "c": k} for d in (1, 2, 3) for k in (c, other)]
     peers += [{"y": plus(y, d)} for d in (1, 2, 3)]
-    peers += [{"zh": plus(z, d, 8) // 4, "zl": plus(z, d, 4)} for d in range(1, 8)]
+    peers += [{"c": other}]
     for peer in peers:
         pl.semaphore_signal(barrier, inc=1, device_id=peer, device_id_type=MESH)
     pl.semaphore_wait(barrier, len(peers))
@@ -146,9 +147,6 @@
     b_copies[1].wait_recv()
     fwd_b = rdma(from_right[1], far[1], b_send.at[5], b_recv.at[5], x=xm)
     fwd_b.start()
-    send_inputs(0)
-    if n_chunks > 1:
-        send_inputs(1)
 
     for copy in ty_copies:
         copy.wait()
@@ -196,9 +194,12 @@
     sib_copies[1].start()
     b_copies[3].wait_recv()
     sib_copies[3].start()
+    send_inputs(0)
     fwd_a.wait_recv()
     fwd_b.wait_recv()
     sib_copies[2].start()
+    for m in range(1, AHEAD):
+        send_inputs(m)
     for copy in sib_copies:
         copy.wait_recv()
 
@@ -221,8 +222,8 @@
     def multiply(m):
         r = rows_of[m]
         await_bytes(ab.at[r], a_recv.at[m])
-        if m + 2 < n_chunks:
-            send_inputs(m + 2)
+        if m + AHEAD < n_chunks:
+            send_inputs(m + AHEAD)
 
         @pl.loop(0, 4)
         def _(q):
@@ -338,33 +339,35 @@
         rdma(nxt.at[theirs], xo_ref, e_send.at[5], e_recv.at[5], c=other),
     )
 
-    s_merge, s_along, s_finish, s_gather, s_pass, s_deliver = SKEW
-    chunks = range(n_chunks)
-    for t in range(n_chunks + s_deliver):
-        if t in chunks:
-            multiply(t)
-        if t - s_merge in chunks:
-            merge(t - s_merge)
-        if t - s_along in chunks:
-            along_z(t - s_along)
-
-        @pl.when(owner)
-        def _():
-            if t - s_finish in chunks:
-                finish(t - s_finish)
-            if t - s_gather in chunks:
-                gather_y(t - s_gather)
-            if t - s_finish == n_chunks - 1:
-                for i in range(7):
-                    k = slice(i * 128, (i + 1) * 128)
-                    nzt[:, k] = zf[k, :].T
-                    nxt[:, k] = xf[k, :].T
-                for copy in (*state_out, *state_away):
-                    copy.start()
-            if t - s_pass in chunks and t - s_pass in RELAY:
-                pass_y(t - s_pass)
-            if t - s_deliver in chunks:
-                deliver(t - s_deliver)
+    def state(m):
+        for i in range(7):
+            k = slice(i * 128, (i + 1) * 128)
+            nzt[:, k] = zf[k, :].T
+            nxt[:, k] = xf[k, :].T
+        for copy in (*state_out, *state_away):
+            copy.start()
+
+    stages = {
+        "multiply": multiply, "merge": merge, "along_z": along_z,
+        "finish": finish, "gather_y": gather_y, "pass_y": pass_y, "deliver": deliver,
+    }
+    order = sorted(
+        (starts[m] / 128 + ready, k, m)
+        for m in range(n_chunks)
+        for k, (stage, ready) in enumerate(READY.items())
+        if stage != "pass_y" or m in RELAY
+    )
+    names = list(READY)
+    for _, k, m in order:
+        if k < 3:
+            stages[names[k]](m)
+        else:
+
+            @pl.when(owner)
+            def _():
+                stages[names[k]](m)
+                if names[k] == "finish" and m == n_chunks - 1:
+                    state(m)
 
     for copy in (*b_copies, fwd_a, fwd_b, *sib_copies):
         copy.wait_send()

time: 98.9 us -> 98.6 us (level)
  no operation moved by 1% of the time
where the time goes in v3:
time: 98.6 us; the launch traced here: 98.5 us
  Pallas kernels  94 us (95%)
  local copies, waits for them, and re-layouts  3.21 us (3%)
  between operations  1.29 us (1%)
    pallas_call x1, Pallas kernels, local(): pl.pallas_call(kernel, name='outer_sync', out_shape=(pltpu.VMEM((64, 896)...  94 us
    unnamed x3, local copies, waits for them, and re-layouts  3.21 us

profile of v3, /device:TPU:1, one launch (start us, length us, event | category | flops | bytes accessed | tf_op | source)
XLA Modules:
  0.0 98.5 jit_solution(10924629407823350912)
XLA Ops:
  1.3 94.0 %outer_sync.1 = (f32[64,896]{1,0:T(8,128)S(1)}, f32[64,896]{1,0:T(8,128)S(1)}, bf16[896,2048]{1,0:T(8,128)(2,1)S(1)}) custom-call(bf16[896,2048]{1,0:T(8,128)(2,1)} %bitcast.9, bf16[128,7168]{1,0:T(8,128)(2,1)} %bitcast.10, bf16[128,2048]{1,0:T(8,128)(2,1)} %bitcast.11, s32[1]{0:T(128)S(6)} %copy.15.n_ref, f32[64,896]{1,0:T(8,128)} %bitcast.12, ...), custom_call_target="tpu_custom_call" | custom-call | flops 3760000000 | bytes 12000000 | tf_op jit(solution)/shard_map/outer_sync/pallas_call | solution.py:407
  95.3 0.7 copy.12
  96.0 0.7 copy.13
  96.7 1.8 %copy.14 = bf16[896,2048]{1,0:T(8,128)(2,1)} copy(bf16[896,2048]{1,0:T(8,128)(2,1)S(1)} %get-tuple-element.11) | data formatting | bytes 7340032

commit v4 on v3

--- a/solution.py
+++ b/solution.py
@@ -10,7 +10,7 @@
 
 ROUND = 3
 MESH = pl.DeviceIdType.MESH
-CHUNKS = (128, 128, 128, 128, 128, 128, 64, 64)
+CHUNKS = (64, 128, 128, 128, 128, 128, 128, 64)
 READY = {"multiply": 0, "merge": 1.01, "along_z": 2.02, "finish": 3.03, "gather_y": 4.04, "pass_y": 5.05, "deliver": 6.06}
 AHEAD = 2
 RELAY = (0, 1, 2, 3, 4, 5)

time: 98.6 us -> 96.6 us (0.980)
  Pallas kernels: 94 us -> 92 us
    pallas_call x1, Pallas kernels: 94 us -> 92 us  [local(): pl.pallas_call(kernel, name='outer_sync', out_shape=(pltpu.VMEM((64, 896)...]
where the time goes in v4:
time: 96.6 us; the launch traced here: 96.5 us
  Pallas kernels  92 us (95%)
  local copies, waits for them, and re-layouts  3.21 us (3%)
  between operations  1.29 us (1%)
    pallas_call x1, Pallas kernels, local(): pl.pallas_call(kernel, name='outer_sync', out_shape=(pltpu.VMEM((64, 896)...  92 us
    unnamed x3, local copies, waits for them, and re-layouts  3.21 us

profile of v4, /device:TPU:1, one launch (start us, length us, event | category | flops | bytes accessed | tf_op | source)
XLA Modules:
  0.0 96.5 jit_solution(8574769359986910537)
XLA Ops:
  1.3 92.0 %outer_sync.1 = (f32[64,896]{1,0:T(8,128)S(1)}, f32[64,896]{1,0:T(8,128)S(1)}, bf16[896,2048]{1,0:T(8,128)(2,1)S(1)}) custom-call(bf16[896,2048]{1,0:T(8,128)(2,1)} %bitcast.9, bf16[128,7168]{1,0:T(8,128)(2,1)} %bitcast.10, bf16[128,2048]{1,0:T(8,128)(2,1)} %bitcast.11, s32[1]{0:T(128)S(6)} %copy.15.n_ref, f32[64,896]{1,0:T(8,128)} %bitcast.12, ...), custom_call_target="tpu_custom_call" | custom-call | flops 3760000000 | bytes 12000000 | tf_op jit(solution)/shard_map/outer_sync/pallas_call | solution.py:407
  93.2 0.7 copy.12
  93.9 0.7 copy.13
  94.6 1.8 %copy.14 = bf16[896,2048]{1,0:T(8,128)(2,1)} copy(bf16[896,2048]{1,0:T(8,128)(2,1)S(1)} %get-tuple-element.11) | data formatting | bytes 7340032

commit v5 on v4

--- a/solution.py
+++ b/solution.py
@@ -10,10 +10,10 @@
 
 ROUND = 3
 MESH = pl.DeviceIdType.MESH
-CHUNKS = (64, 128, 128, 128, 128, 128, 128, 64)
+CHUNKS = (64, 64, 128, 128, 128, 128, 128, 64, 64)
 READY = {"multiply": 0, "merge": 1.01, "along_z": 2.02, "finish": 3.03, "gather_y": 4.04, "pass_y": 5.05, "deliver": 6.06}
 AHEAD = 2
-RELAY = (0, 1, 2, 3, 4, 5)
+RELAY = (0, 1, 2, 3, 4, 5, 6)
 Y_FIRST = ()
 F32 = jnp.float32
 BF16 = jnp.bfloat16

time: 96.6 us -> 98.5 us (1.020)
  Pallas kernels: 92 us -> 93.9 us
    pallas_call x1, Pallas kernels: 92 us -> 93.9 us  [local(): pl.pallas_call(kernel, name='outer_sync', out_shape=(pltpu.VMEM((64, 896)...]
where the time goes in v5:
time: 98.5 us; the launch traced here: 98.4 us
  Pallas kernels  93.9 us (95%)
  local copies, waits for them, and re-layouts  3.21 us (3%)
  between operations  1.29 us (1%)
    pallas_call x1, Pallas kernels, local(): pl.pallas_call(kernel, name='outer_sync', out_shape=(pltpu.VMEM((64, 896)...  93.9 us
    unnamed x3, local copies, waits for them, and re-layouts  3.21 us

profile of v5, /device:TPU:1, one launch (start us, length us, event | category | flops | bytes accessed | tf_op | source)
XLA Modules:
  0.0 98.4 jit_solution(12225548507872227697)
XLA Ops:
  1.3 93.9 %outer_sync.1 = (f32[64,896]{1,0:T(8,128)S(1)}, f32[64,896]{1,0:T(8,128)S(1)}, bf16[896,2048]{1,0:T(8,128)(2,1)S(1)}) custom-call(bf16[896,2048]{1,0:T(8,128)(2,1)} %bitcast.9, bf16[128,7168]{1,0:T(8,128)(2,1)} %bitcast.10, bf16[128,2048]{1,0:T(8,128)(2,1)} %bitcast.11, s32[1]{0:T(128)S(6)} %copy.15.n_ref, f32[64,896]{1,0:T(8,128)} %bitcast.12, ...), custom_call_target="tpu_custom_call" | custom-call | flops 3760000000 | bytes 12000000 | tf_op jit(solution)/shard_map/outer_sync/pallas_call | solution.py:407
  95.2 0.7 copy.12
  95.9 0.7 copy.13
  96.6 1.8 %copy.14 = bf16[896,2048]{1,0:T(8,128)(2,1)} copy(bf16[896,2048]{1,0:T(8,128)(2,1)S(1)} %get-tuple-element.11) | data formatting | bytes 7340032
